TPU v7x, 32 devices: a whole 2x2x4 slice. The times are simulated.
32 devices in a mesh: dp: 8 (over z, x), tensor: 4 (over y, core).
Axes of the slice: x: 2, y: 2, z: 4, core: 2. Of those that a mesh axis runs over, the one named last changes fastest.
Arguments:
- tokens: bfloat16 [16384, 1024], P(('dp', 'tensor')), may hold values from -6 to 6
- out_grad: bfloat16 [16384, 1024], P(('dp', 'tensor')), may hold values from -6 to 6
- seq_lengths: int32 [16], P('dp'), may hold values from 256 to 1024, as said below
- norm_gains: float32 [2, 1024], replicated, may hold values from 0.25 to 1.75
- row_biases: float32 [4, 1024], replicated, may hold values from -1.5 to 1.5
- qkv_weight: bfloat16 [1024, 3072], P('dp', 'tensor'), may hold values from -0.1875 to 0.1875
- qkv_bias: float32 [3072], P('tensor'), may hold values from -2.5 to 2.5
- dense_weight: bfloat16 [1024, 1024], P('tensor', 'dp'), may hold values from -0.75 to 0.75
- fc1_weight: bfloat16 [1024, 4096], P('dp', 'tensor'), may hold values from -0.1875 to 0.1875
- fc1_bias: float32 [4096], P('tensor'), may hold values from -2.5 to 2.5
- fc2_weight: bfloat16 [4096, 1024], P('tensor', 'dp'), may hold values from -0.09375 to 0.09375
- block_slot: int32 [768], replicated, may hold values from 0 to 767, as said below
- left_stat: float32 [768, 128, 128], P(('dp', 'tensor'))
- right_stat: float32 [768, 128, 128], P(('dp', 'tensor'))
- left_root: float32 [768, 128, 128], P(('dp', 'tensor'))
- right_root: float32 [768, 128, 128], P(('dp', 'tensor'))
- row_accum: float32 [6, 1024], replicated, may hold values from 0.5 to 2
- qkv_bias_accum: float32 [3072], P('tensor'), may hold values from 0.5 to 2
- fc1_bias_accum: float32 [4096], P('tensor'), may hold values from 0.5 to 2
Outputs:
- layer_out: bfloat16 [16384, 1024], P(('dp', 'tensor'))
- input_grad: float32 [16384, 1024], P(('dp', 'tensor'))
- block_grad: float32 [768, 128, 128], P(('dp', 'tensor'))
- left_new: float32 [768, 128, 128], P(('dp', 'tensor'))
- right_new: float32 [768, 128, 128], P(('dp', 'tensor'))
- block_update: float32 [768, 128, 128], P(('dp', 'tensor'))
- row_accum_new: float32 [6, 1024], replicated
- row_update: float32 [6, 1024], replicated
- qkv_bias_accum_new: float32 [3072], P('tensor')
- qkv_bias_update: float32 [3072], P('tensor')
- fc1_bias_accum_new: float32 [4096], P('tensor')
- fc1_bias_update: float32 [4096], P('tensor')
Inputs may be any that keep to these rules, and one draw needn't show every extreme that they name: `seq_lengths`: some sequence has exactly 1024 real tokens. `block_slot`: a permutation of the 768 slots; block t * 192 + j gets a slot s for which (s // 24) modulo the tensor axis's size is t.
All inputs are finite; a program needn't handle non-finite values.
Results may differ from a plain program's by a relative error of at most 0.0088.
Values may be sent and summed in bfloat16 or wider, within the bound.
A program may use at most 192 MiB of HBM per device.

v0:
```python
import functools
import math

import jax
import jax.numpy as jnp
import numpy as np
from jax import lax
from jax.experimental import pallas as pl
from jax.experimental.pallas import tpu as pltpu
from jax.sharding import PartitionSpec as P

HEAD = 64
ROT = 16
LEN = 1024
BLOCK = 128
TILE = 256
WIDE = 512
MESH = pl.DeviceIdType.MESH
VMEM_LIMIT = 60 * 1024 * 1024

masked_score = -1e30
shampoo_rate = 0.03
adagrad_rate = 0.1
stat_decay = 0.5
f32 = jnp.float32
bf16 = jnp.bfloat16


def rotary_rows():
    half = ROT // 2
    inverse = np.power(np.float32(10000.0), -(np.arange(half, dtype=np.float32) * np.float32(2.0 / ROT)))
    angles = inverse.astype(np.float32)[:, None] * np.arange(LEN, dtype=np.float32)[None, :]
    return np.concatenate([np.cos(angles), np.sin(angles)], axis=0).astype(np.float32)


def ring_place(me, count):
    low, high = me % 2, me // 2
    return low * (count - 1 - high) + (1 - low) * high


def ring_device(place, count):
    upper = place // (count // 2)
    return (1 - upper) * (2 * place) + upper * (2 * (count - 1 - place) + 1)


def hop_count(half, way, count):
    far = count // 2
    return far if half == way else far - 1


def for_hops(first, last, body, count):
    if count <= 8:
        for hop in range(first, last):
            body(hop)
    elif last > first:

        @pl.loop(first, last)
        def _(hop):
            body(hop)


def as_rows(vec):
    return vec.reshape(-1, BLOCK)


def as_line(rows):
    return jnp.concatenate([rows[k : k + 1, :] for k in range(rows.shape[0])], axis=1)


class Ring:
    def __init__(self, count):
        self.count = count
        self.me = lax.axis_index("dp")
        self.tensor = lax.axis_index("tensor")
        self.place = ring_place(self.me, count)
        self.peer = [
            (ring_device((self.place + step) % count, count), self.tensor) for step in (1, count - 1)
        ]

    def at(self, offset):
        return ring_device((self.place + offset + 2 * self.count) % self.count, self.count)


class Gather:
    def __init__(self, ring, locals_, fulls, send, recv):
        self.ring, self.locals, self.fulls, self.send, self.recv = ring, locals_, fulls, send, recv
        self.far = ring.count // 2

    def part(self, ref, w, half, owner=None):
        rows, cols = self.locals[w].shape
        base = 0 if owner is None else owner * rows
        if rows % 32 == 0:
            return ref.at[pl.ds(pl.multiple_of(base + half * (rows // 2), 16), rows // 2)]
        return ref.at[pl.ds(base, rows), pl.ds(half * (cols // 2), cols // 2)]

    def sem(self, w, half, way, hop):
        return ((w * 2 + half) * 2 + way) * self.far + hop - 1

    def copy(self, w, half, way, hop, source):
        owner = self.ring.at((1 - hop) if way == 0 else (hop - 1))
        src = self.part(self.locals[w], w, half) if source else self.part(self.fulls[w], w, half, owner)
        return pltpu.make_async_remote_copy(
            src_ref=src,
            dst_ref=self.part(self.fulls[w], w, half, owner),
            send_sem=self.send.at[self.sem(w, half, way, hop)],
            recv_sem=self.recv.at[self.sem(w, half, way, hop)],
            device_id=self.ring.peer[way],
            device_id_type=MESH,
        )

    def arrival(self, w, half, way, hop):
        owner = self.ring.at(-hop if way == 0 else hop)
        dst = self.part(self.fulls[w], w, half, owner)
        return pltpu.make_async_remote_copy(
            src_ref=dst,
            dst_ref=dst,
            send_sem=self.send.at[self.sem(w, half, way, hop)],
            recv_sem=self.recv.at[self.sem(w, half, way, hop)],
            device_id=self.ring.peer[way],
            device_id_type=MESH,
        )

    def begin(self, w):
        for half in range(2):
            for way in range(2):
                if hop_count(half, way, self.ring.count) >= 1:
                    self.copy(w, half, way, 1, True).start()

    def forward(self, w, hop, last):
        for half in range(2):
            for way in range(2):
                hops = self.far if half == way else self.far - 1
                if last and hops != self.far:
                    continue
                self.arrival(w, half, way, hop).wait_recv()
                if not last:
                    more = self.far if half == way else self.far - 1
                    if more == self.far:
                        self.copy(w, half, way, hop + 1, False).start()
                    else:

                        @pl.when(hop + 1 <= more)
                        def _():
                            self.copy(w, half, way, hop + 1, False).start()

    def finish(self, w):
        for half in range(2):
            for way in range(2):
                hops = hop_count(half, way, self.ring.count)
                if hops >= 1:
                    self.copy(w, half, way, 1, True).wait_send()
                for_hops(
                    2, hops + 1, lambda hop: self.copy(w, half, way, hop, False).wait_send(), self.ring.count
                )


class Rows:
    def __init__(self, local, full, send, recv, own):
        self.tensor = lax.axis_index("tensor")
        self.dp = lax.axis_index("dp")
        self.near = self.tensor + 1 - 2 * (self.tensor % 2)
        self.across = (self.tensor + 2) % 4
        self.local, self.full, self.send, self.recv, self.own = local, full, send, recv, own
        self.rows = local.shape[0]

    def slot(self, owner, piece=None):
        if piece is None:
            return self.full.at[pl.ds(pl.multiple_of(owner * self.rows, 16), self.rows)]
        half = self.rows // 2
        return self.full.at[pl.ds(pl.multiple_of(owner * self.rows + piece * half, 16), half)]

    def remote(self, src, dst, sem, device):
        return pltpu.make_async_remote_copy(
            src_ref=src,
            dst_ref=dst,
            send_sem=self.send.at[sem],
            recv_sem=self.recv.at[sem],
            device_id=(self.dp, device),
            device_id_type=MESH,
        )

    def keep(self):
        return pltpu.make_async_copy(self.local, self.slot(self.tensor), self.own)

    def pair(self):
        return self.remote(self.local, self.slot(self.tensor), 0, self.near)

    def cross(self, piece):
        half = self.rows // 2
        return self.remote(
            self.local.at[pl.ds(piece * half, half)], self.slot(self.tensor, piece), 1 + piece, self.across
        )

    def onward(self, piece):
        here = self.slot(self.across, piece)
        return self.remote(here, here, 3 + piece, self.near)

    def begin_near(self):
        self.keep().start()
        self.pair().start()

    def begin_cross(self):
        for piece in range(2):
            self.cross(piece).start()

    def pass_piece(self, piece):
        self.cross(piece).wait_recv()
        self.onward(piece).start()

    def pass_on(self):
        for piece in range(2):
            self.pass_piece(piece)

    def finish(self):
        self.keep().wait()
        self.pair().wait()
        for piece in range(2):
            self.cross(piece).wait_send()
            self.onward(piece).wait()


def greet(devices):
    barrier = pltpu.get_barrier_semaphore()
    for device in devices:
        pl.semaphore_signal(barrier, inc=1, device_id=device, device_id_type=MESH)
    pl.semaphore_wait(barrier, len(devices))


def dot_nn(a, b):
    return lax.dot_general(a, b, (((1,), (0,)), ((), ())), preferred_element_type=f32)


def dot_nt(a, b):
    return lax.dot_general(a, b, (((1,), (1,)), ((), ())), preferred_element_type=f32)


def dot_tn(a, b):
    return lax.dot_general(a, b, (((0,), (0,)), ((), ())), preferred_element_type=f32)


def normed(x):
    average = jnp.mean(x, axis=-1, keepdims=True)
    centered = x - average
    variance = jnp.mean(centered * centered, axis=-1, keepdims=True)
    scale = lax.rsqrt(variance + 1e-05)
    return centered * scale, scale


def mixed_kernel(
    count, lim_ref, gain_ref, bias_ref, qb_ref, rot_ref, slot_ref, wd, w2, x, dy, wq, w1,
    x_out, h1_out, dyb_out, ctx_out, dproj_out, wqd_out, w1f, w2f, sum_ref, order_ref,
    xf, dyf, wf, wl, w2l, h1s, ctxs, dps, qt, kt, vt, dct, ctt, dqt, kr, vr, dkvs,
    rs, rr, ro, gs, gr, go, os,
):
    ring = Ring(count)
    pair_cols = 6 * HEAD
    half_cols = pair_cols + 2 * HEAD
    parts = [
        pltpu.make_async_copy(
            wq.at[:, pl.ds(p * pair_cols, pair_cols)], wl.at[:, pl.ds(p * half_cols, pair_cols)], os.at[p]
        )
        for p in range(2)
    ]
    for copy in parts:
        copy.start()
    turned_dense = wd[...].T
    for p in range(2):
        wl[:, p * half_cols + pair_cols : (p + 1) * half_cols] = turned_dense[:, p * 2 * HEAD : (p + 1) * 2 * HEAD]
    views = [(wl.at[:, pl.ds(p * half_cols, half_cols)], wf.at[:, pl.ds(p * half_cols, half_cols)]) for p in (0, 1)]
    views += [(w1, w1f), (w2l, w2f)]
    gather = Gather(ring, [v[0] for v in views], [v[1] for v in views], gs, gr)
    rx = Rows(x, xf, rs.at[0], rr.at[0], ro.at[0])
    ry = Rows(dy, dyf, rs.at[1], rr.at[1], ro.at[1])
    greet([ring.peer[0], ring.peer[1], (ring.me, rx.near), (ring.me, rx.across)])
    far = count // 2
    own = []
    for k, (local, full) in enumerate(((w1, w1f), (w2l, w2f))):
        rows = local.shape[0]
        own.append(
            pltpu.make_async_copy(local, full.at[pl.ds(pl.multiple_of(ring.me * rows, 16), rows)], go.at[k])
        )
    rx.begin_near()
    for copy in parts:
        copy.wait()
    gather.begin(0)
    rx.begin_cross()
    ry.begin_near()
    ry.begin_cross()
    wf[pl.ds(pl.multiple_of(ring.me * wl.shape[0], 16), wl.shape[0]), :] = wl[...]
    own[0].start()
    sum_ref[...] = jnp.zeros_like(sum_ref)
    tensor = ring.tensor
    tiles = LEN // TILE

    def whole_ring(w):
        for_hops(1, far, lambda hop: gather.forward(w, hop, False), count)
        gather.forward(w, far, True)

    def hop_at(w, hop):
        if count == 8:
            gather.forward(w, hop, hop == far)
        elif hop == 4:
            whole_ring(w)

    def rows_of(seq, i):
        return pl.ds(pl.multiple_of(seq * LEN + i * TILE, TILE), TILE)

    def norm_tile(seq, i):
        rows = rows_of(seq, i)
        xhat, _ = normed(xf[rows, :].astype(f32))
        h1s[rows, :] = (xhat * gain_ref[0:1, :] + bias_ref[0:1, :]).astype(bf16)

    def mask_tile(seq, i):
        rows = rows_of(seq, i)
        place = i * TILE + lax.broadcasted_iota(jnp.int32, (TILE, 1), 0)
        kept = jnp.where(place < lim_ref[seq], dyf[rows, :].astype(f32), 0.0)
        sum_ref[4:5, :] += jnp.sum(kept, axis=0, keepdims=True)
        dyf[rows, :] = kept.astype(bf16)

    def turned(first, second, cosine, sine):
        return first * cosine - second * sine, second * cosine + first * sine

    def prepare_tile(seq, pair, i):
        rows = rows_of(seq, i)
        cols = pl.ds(pl.multiple_of(i * TILE, TILE), TILE)
        proj = dot_nn(h1s[rows, :], wf[:, pl.ds(pl.multiple_of(pair * half_cols, BLOCK), pair_cols)])
        proj = proj + as_line(qb_ref[pl.ds(pair * (pair_cols // BLOCK), pair_cols // BLOCK), :])
        proj = proj.T
        cosine, sine = rot_ref[0:8, cols], rot_ref[8:16, cols]
        key = i * TILE + lax.broadcasted_iota(jnp.int32, (16, TILE), 1)
        row = lax.broadcasted_iota(jnp.int32, (16, TILE), 0)
        ones = jnp.where(row == 0, 1.0, 0.0).astype(bf16)
        hidden = jnp.where((row == 0) & (key >= lim_ref[seq]), masked_score, 0.0).astype(bf16)
        blank = jnp.zeros((48, TILE), bf16)
        none = jnp.zeros((HEAD, TILE), bf16)
        for hh in range(2):
            h = 2 * pair + hh
            base = 3 * HEAD * hh
            q0, q1 = turned(proj[base : base + 8], proj[base + 8 : base + 16], cosine, sine)
            q = jnp.concatenate([q0, q1, proj[base + 16 : base + HEAD]], axis=0).astype(bf16)
            q = (q.astype(f32) * 0.125).astype(bf16)
            qt[h, :, cols] = jnp.concatenate([q, ones, blank], axis=0)
            base += HEAD
            k0, k1 = turned(proj[base : base + 8], proj[base + 8 : base + 16], cosine, sine)
            k = jnp.concatenate([k0, k1, proj[base + 16 : base + HEAD]], axis=0).astype(bf16)
            kt[h, :, cols] = k
            kr[h, cols, :] = jnp.concatenate([k, hidden, blank], axis=0).T
            base += HEAD
            v = proj[base : base + HEAD].astype(bf16)
            vt[h, :, cols] = jnp.concatenate([v, ones], axis=0)
            vr[h, cols, :] = jnp.concatenate([none, v], axis=0).T

    def context_tile(seq, pair, i):
        cols = pl.ds(pl.multiple_of(i * TILE, TILE), TILE)
        begin = pair * half_cols + pair_cols
        dctx = dot_nn(dyf[rows_of(seq, i), :], wf[:, begin : begin + 2 * HEAD]).T.astype(bf16)
        for hh in range(2):
            dct[2 * pair + hh, :, cols] = dctx[HEAD * hh : HEAD * (hh + 1)]

    def back_tile(seq, i):
        mask_tile(seq, i)
        context_tile(seq, 0, i)
        context_tile(seq, 1, i)

    def attend(pair, i, fresh):
        here = slice(i * TILE, (i + 1) * TILE)
        chunks = [slice(c * TILE, (c + 1) * TILE) for c in range(i + 1)]
        heads = range(2)
        of = [2 * pair, 2 * pair + 1]
        key = lax.broadcasted_iota(jnp.int32, (TILE, TILE), 0)
        query = lax.broadcasted_iota(jnp.int32, (TILE, TILE), 1)
        q = [qt[of[hh], :, here] for hh in heads]
        scores = [[dot_nn(kr[of[hh], c, :], q[hh]) for c in chunks] for hh in heads]
        probs, grads, deltas, both = [], [], [], []
        none = jnp.zeros((HEAD, TILE), bf16)
        for hh in heads:
            scores[hh][i] = jnp.where(key <= query, scores[hh][i], masked_score)
            top = jnp.max(scores[hh][0], axis=0, keepdims=True)
            for s in scores[hh][1:]:
                top = jnp.maximum(top, jnp.max(s, axis=0, keepdims=True))
            probs.append([jnp.exp(s - top).astype(bf16) for s in scores[hh]])
        for hh in heads:
            total = dot_nn(vt[of[hh], :, chunks[0]], probs[hh][0])
            for c, p in zip(chunks[1:], probs[hh][1:]):
                total = total + dot_nn(vt[of[hh], :, c], p)
            inverse = 1.0 / total[HEAD : HEAD + 1]
            context = total[:HEAD] * inverse
            ctt[of[hh], :, here] = context
            grad = (dct[of[hh], :, here].astype(f32) * inverse).astype(bf16)
            deltas.append(jnp.sum(grad.astype(f32) * context, axis=0, keepdims=True))
            grad = jnp.concatenate([none, grad], axis=0)
            grads.append(grad)
            both.append(jnp.concatenate([jnp.concatenate([q[hh][:HEAD], none], axis=0), grad], axis=1))
        dq = [None, None]
        for n, c in enumerate(chunks):
            for hh in heads:
                p = probs[hh][n]
                dp = dot_nn(vr[of[hh], c, :], grads[hh])
                ds = (p.astype(f32) * (dp - deltas[hh])).astype(bf16)
                part = dot_nn(kt[of[hh], :, c], ds)
                dq[hh] = part if dq[hh] is None else dq[hh] + part
                dkv = dot_nt(jnp.concatenate([ds, p], axis=1), both[hh])
                if n in fresh:
                    dkvs[of[hh], c, :] = dkv
                else:
                    dkvs[of[hh], c, :] += dkv
        for hh in heads:
            dqt[of[hh], :, here] = dq[hh] * 0.125

    def collect_tile(seq, i):
        rows = rows_of(seq, i)
        cols = pl.ds(pl.multiple_of(i * TILE, TILE), TILE)
        cosine, sine = rot_ref[0:8, cols], rot_ref[8:16, cols]
        for pair in range(2):
            pieces = []
            for h in (2 * pair, 2 * pair + 1):
                dkv = dkvs[h, cols, :].T
                for grad in (dqt[h, :, cols], dkv[:HEAD]):
                    pieces += [*turned(grad[0:8], grad[8:16], cosine, -sine), grad[16:HEAD]]
                pieces.append(dkv[HEAD:])
            low = jnp.concatenate(pieces, axis=0).T.astype(bf16)
            wide = slice(pair * pair_cols, (pair + 1) * pair_cols)
            dps[rows, wide] = low
            sum_ref[5:6, wide] += jnp.sum(low.astype(f32), axis=0, keepdims=True)
            ctx = jnp.concatenate([ctt[2 * pair, :, cols], ctt[2 * pair + 1, :, cols]], axis=0).T
            ctxs[rows, pair * 2 * HEAD : (pair + 1) * 2 * HEAD] = ctx.astype(bf16)

    def save(turn, k, seq):
        src, dst = ((xf, x_out), (h1s, h1_out), (dyf, dyb_out), (ctxs, ctx_out), (dps, dproj_out))[k]
        rows = pl.ds(pl.multiple_of(seq * LEN, LEN), LEN)
        return pltpu.make_async_copy(src.at[rows], dst.at[rows], os.at[turn * 5 + k])

    mine = order_ref.shape[1]
    per = mine // count
    place = lax.broadcasted_iota(jnp.int32, (mine, 1), 0).astype(f32)
    owner = jnp.floor((place + 0.5) / per)
    wanted = (owner * 4.0 + lax.convert_element_type(tensor, f32)) * per + (place - owner * per)
    found = jnp.zeros(order_ref.shape, f32)
    for r in range(slot_ref.shape[0]):
        hit = jnp.where(slot_ref[r : r + 1, :].astype(f32) == wanted, 1.0, 0.0).astype(bf16)
        block = r * BLOCK + lax.broadcasted_iota(jnp.int32, (8, BLOCK), 1) - tensor * mine
        found = found + dot_nt(jnp.clip(block, 0, mine - 1).astype(f32).astype(bf16), hit)
    order_ref[...] = (found + 0.5).astype(jnp.int32)

    seq = tensor // 2
    rx.keep().wait()
    rx.pair().wait_recv()

    @pl.loop(0, tiles)
    def _(i):
        norm_tile(seq, i)

        @pl.when(i == 0)
        def _():
            hop_at(0, 1)
            gather.begin(1)

        @pl.when(i == 1)
        def _():
            hop_at(0, 2)
            hop_at(1, 1)

        @pl.when(i == 2)
        def _():
            hop_at(0, 3)
            hop_at(1, 2)
            gather.begin(2)

    save(0, 0, seq).start()
    save(0, 1, seq).start()
    w2l[...] = w2[...].T
    hop_at(0, 4)
    ry.keep().wait()
    ry.pair().wait_recv()

    @pl.loop(0, tiles // 2)
    def _(i):
        for sub in range(2):
            prepare_tile(seq, 0, 2 * i + sub)


    @pl.loop(0, tiles)
    def _(i):
        mask_tile(seq, i)
        context_tile(seq, 0, i)

    save(0, 2, seq).start()

    @pl.loop(0, 2)
    def _(pair):
        @pl.when(pair == 1)
        def _():
            hop_at(1, 4)
            hop_at(2, 1)

            @pl.loop(0, tiles // 2)
            def _(i):
                for sub in range(2):
                    prepare_tile(seq, 1, 2 * i + sub)
                    context_tile(seq, 1, 2 * i + sub)

        attend(pair, 3, (0, 1, 2, 3))

        @pl.when(pair == 0)
        def _():
            hop_at(1, 3)
            gather.begin(3)
            own[1].start()

        attend(pair, 2, ())

        @pl.when(pair == 0)
        def _():
            rx.pass_on()

        @pl.when(pair == 1)
        def _():
            hop_at(3, 1)

        attend(pair, 1, ())
        attend(pair, 0, ())

    @pl.loop(0, tiles)
    def _(i):
        collect_tile(seq, i)

    save(0, 3, seq).start()
    save(0, 4, seq).start()
    keep = pltpu.make_async_copy(wf, wqd_out, os.at[10])
    keep.start()

    seq = 1 - seq
    for piece in range(2):
        rx.onward(piece).wait_recv()

    @pl.loop(0, tiles)
    def _(i):
        norm_tile(seq, i)

    save(1, 0, seq).start()
    save(1, 1, seq).start()
    ry.pass_piece(0)

    for pair in range(2):

        @pl.loop(0, tiles // 2)
        def _(i):
            for sub in range(2):
                prepare_tile(seq, pair, 2 * i + sub)

        if pair == 0:
            hop_at(2, 2)

    ry.onward(0).wait()
    back_tile(seq, 0)
    back_tile(seq, 2)

    @pl.loop(0, 2)
    def _(pair):
        attend(pair, 2, (0, 1, 2))

        @pl.when(pair == 0)
        def _():
            hop_at(3, 2)

        attend(pair, 0, ())

    ry.pass_piece(1)
    ry.onward(1).wait()
    back_tile(seq, 1)
    back_tile(seq, 3)
    save(1, 2, seq).start()
    hop_at(2, 3)

    @pl.loop(0, 2)
    def _(pair):
        attend(pair, 3, (3,))

        @pl.when(pair == 1)
        def _():
            hop_at(3, 3)

        attend(pair, 1, ())

    @pl.loop(0, tiles)
    def _(i):
        collect_tile(seq, i)

    save(1, 3, seq).start()
    save(1, 4, seq).start()
    hop_at(2, 4)
    hop_at(3, 4)
    for w in range(4):
        gather.finish(w)
    own[0].wait()
    own[1].wait()
    rx.pair().wait_send()
    ry.pair().wait_send()
    for piece in range(2):
        rx.cross(piece).wait_send()
        rx.onward(piece).wait_send()
        ry.cross(piece).wait_send()
    for turn in range(2):
        for k in range(5):
            save(turn, k, turn + (1 - 2 * turn) * (tensor // 2)).wait()
    keep.wait()


def mixed_all(count, limits, gains, biases, qkv_bias, rot, slots, x, dy, wq, wd, w1, w2):
    far = count // 2
    rows, width = 4 * x.shape[0], x.shape[1]
    ctx_cols, proj_cols = wd.shape[0], wq.shape[1]
    shard = wq.shape[0]
    out = lambda r, c: jax.ShapeDtypeStruct((r, c), bf16)
    any_, vmem = pl.BlockSpec(memory_space=pl.ANY), pl.BlockSpec(memory_space=pltpu.VMEM)
    dma = lambda *n: pltpu.SemaphoreType.DMA(n)
    buf = lambda dtype, *shape: pltpu.VMEM(shape, dtype)
    heads, both = 4, ctx_cols + proj_cols
    return pl.pallas_call(
        functools.partial(mixed_kernel, count),
        out_shape=[
            out(rows, width), out(rows, width), out(rows, width), out(rows, ctx_cols), out(rows, proj_cols),
            out(width, both), out(width, w1.shape[1]), out(width, w2.shape[0]),
            jax.ShapeDtypeStruct((8, width), f32), jax.ShapeDtypeStruct((8, slots.size // 4), jnp.int32),
        ],
        in_specs=[pl.BlockSpec(memory_space=pltpu.SMEM)] + [vmem] * 7 + [any_] * 4,
        out_specs=[any_] * 8 + [vmem] * 2,
        scratch_shapes=[
            buf(bf16, rows, width), buf(bf16, rows, width), buf(bf16, width, both),
            buf(bf16, shard, both), buf(bf16, shard, w2.shape[0]),
            buf(bf16, rows, width), buf(bf16, rows, ctx_cols), buf(bf16, rows, proj_cols),
            buf(bf16, heads, 2 * HEAD, LEN), buf(bf16, heads, HEAD, LEN), buf(bf16, heads, HEAD + 16, LEN),
            buf(bf16, heads, HEAD, LEN), buf(f32, heads, HEAD, LEN), buf(f32, heads, HEAD, LEN),
            buf(bf16, heads, LEN, 2 * HEAD), buf(bf16, heads, LEN, 2 * HEAD), buf(f32, heads, LEN, 2 * HEAD),
            dma(2, 5), dma(2, 5), dma(2), dma(16 * far), dma(16 * far), dma(2), dma(11),
        ],
        compiler_params=pltpu.CompilerParams(
            collective_id=0, has_side_effects=True, vmem_limit_bytes=VMEM_LIMIT
        ),
        cost_estimate=pl.CostEstimate(flops=int(2e10), bytes_accessed=int(4e7), transcendentals=int(1e7)),
        name="mixed_all",
    )(limits, gains, biases, qkv_bias, rot, slots, wd, w2, x, dy, wq, w1)


def gelu_both(x):
    bell = jnp.exp(-0.5 * x * x)
    u = jnp.abs(x) * (1.0 / math.sqrt(2.0))
    t = 1.0 / (1.0 + 0.3275911 * u)
    poly = t * (0.254829592 + t * (-0.284496736 + t * (1.421413741 + t * (-1.453152027 + t * 1.061405429))))
    tail = 0.5 * poly * bell
    phi = jnp.where(x < 0.0, tail, 1.0 - tail)
    return x * phi, phi + x * bell * (1.0 / math.sqrt(2.0 * math.pi))


class Scatter:
    def __init__(self, ring, order, blocks, out, sbuf, rbuf, send, recv):
        self.ring, self.order, self.blocks, self.out = ring, order, blocks, out
        self.sbuf, self.rbuf, self.send, self.recv = sbuf, rbuf, send, recv
        self.per = out.shape[0]
        self.far = ring.count // 2

    def index(self, half, way, hop):
        return (half * 2 + way) * self.far + hop - 1

    def copy(self, half, way, hop, first):
        i = self.index(half, way, hop)
        return pltpu.make_async_remote_copy(
            src_ref=self.sbuf.at[half * 2 + way] if first else self.rbuf.at[i - 1],
            dst_ref=self.rbuf.at[i],
            send_sem=self.send.at[i],
            recv_sem=self.recv.at[i],
            device_id=self.ring.peer[way],
            device_id_type=MESH,
        )

    def own(self, dest, half, k):
        return self.blocks[self.order[0, dest * self.per + k], half * 64 : half * 64 + 64, :].astype(f32)

    def step(self, half, way, hop, first):
        hops = hop_count(half, way, self.ring.count)
        dest = self.ring.at((hops + 1 - hop) if way == 0 else (hop - hops - 1))
        i = self.index(half, way, hop)
        if not first:
            self.copy(half, way, hop - 1, True).wait_recv()

        def one(k, carry):
            value = self.own(dest, half, k)
            if first:
                self.sbuf[half * 2 + way, k] = value.astype(bf16)
            else:
                self.rbuf[i - 1, k] = (value + self.rbuf[i - 1, k].astype(f32)).astype(bf16)
            return carry

        lax.fori_loop(0, self.per, one, 0)
        self.copy(half, way, hop, first).start()

    def last(self, half, scale):
        came = []
        for way in range(2):
            hops = hop_count(half, way, self.ring.count)
            if hops >= 1:
                self.copy(half, way, hops, True).wait_recv()
                came.append(self.index(half, way, hops))
        me = self.ring.me

        def one(k, carry):
            value = self.own(me, half, k)
            for i in came:
                value = value + self.rbuf[i, k].astype(f32)
            self.out[k, half * 64 : half * 64 + 64, :] = value * scale
            return carry

        lax.fori_loop(0, self.per, one, 0)

    def finish(self):
        for half in range(2):
            for way in range(2):
                hops = hop_count(half, way, self.ring.count)
                for_hops(
                    1, hops + 1, lambda hop: self.copy(half, way, hop, True).wait_send(), self.ring.count
                )


class RowSum:
    def __init__(self, parts, r1, base, r2, send, recv):
        self.tensor = lax.axis_index("tensor")
        self.dp = lax.axis_index("dp")
        self.near = self.tensor + 1 - 2 * (self.tensor % 2)
        self.across = (self.tensor + 2) % 4
        self.r2, self.send, self.recv = r2, send, recv
        self.rows = r2.shape[0]
        self.parts = [parts.at[pl.ds(k * self.rows, self.rows)] for k in range(4)]
        self.r1 = [r1.at[pl.ds((base + k) * self.rows, self.rows)] for k in range(2)]

    def remote(self, src, dst, sem, device):
        return pltpu.make_async_remote_copy(
            src_ref=src, dst_ref=dst, send_sem=self.send.at[sem], recv_sem=self.recv.at[sem],
            device_id=(self.dp, device), device_id_type=MESH,
        )

    def pair(self, k):
        return self.remote(self.parts[2 * k], self.r1[k], k, self.near)

    def cross(self):
        return self.remote(self.parts[1], self.r2, 2, self.across)

    def middle(self):
        self.pair(0).wait_recv()
        self.parts[1][...] = (self.parts[1][...].astype(f32) + self.r1[0][...].astype(f32)).astype(bf16)

    def end(self, stage, out, sem):
        self.pair(1).wait_recv()
        self.cross().wait_recv()
        step = stage.shape[1]
        copies = []
        for k in range(self.rows // step):
            at = pl.ds(k * step, step)
            if k >= 2:
                copies[k - 2].wait()
            stage[k % 2] = (
                self.parts[3][at, :].astype(f32) + self.r1[1][at, :].astype(f32) + self.r2[at, :].astype(f32)
            )
            copies.append(pltpu.make_async_copy(stage.at[k % 2], out.at[at], sem.at[k % 2]))
            copies[-1].start()
        for copy in copies[-2:]:
            copy.wait()

    def finish(self):
        self.pair(0).wait_send()
        self.pair(1).wait_send()
        self.cross().wait_send()


def tail_kernel(
    count, scale, order, gain_ref, bias_ref, fb_ref, small_a, x, h1, dyb, ctx, dproj, wqd, w1, w2,
    grad, small_sum, br_out, e_out,
    xs, h1s, dys, cs, ps, wqds, w1s, w2s, h2s, acts, dabs, gs, sbuf, rbuf, r2, stage, small, t_in, d_in, d_out,
    sem, late_sem, ss, sr, rs, rr, ts, tr, ds, dr, os, free,
):
    ring = Ring(count)
    me, tensor = ring.me, ring.tensor
    rows = r2.shape[1]
    tiles = x.shape[0] // WIDE
    near = tensor + 1 - 2 * (tensor % 2)

    barrier = pltpu.get_barrier_semaphore()
    for step in range(1, 4):
        pl.semaphore_signal(barrier, inc=1, device_id=(me, (tensor + step) % 4), device_id_type=MESH)

    @pl.loop(1, count)
    def _(step):
        pl.semaphore_signal(barrier, inc=1, device_id=((me + step) % count, tensor), device_id_type=MESH)

    def tile_copy(k, src, dst, i):
        at = pl.ds(pl.multiple_of(i * WIDE, WIDE), WIDE)
        return pltpu.make_async_copy(src.at[at], dst.at[at], sem.at[k, i])

    late = [
        pltpu.make_async_copy(src, dst, late_sem.at[k])
        for k, (src, dst) in enumerate(((w1, w1s), (w2, w2s), (h1, h1s), (ctx, cs), (dproj, ps), (wqd, wqds)))
    ]
    late[0].start()
    tile_copy(0, x, xs, 0).start()
    late[1].start()
    tile_copy(1, dyb, dys, 0).start()
    for i in range(1, tiles):
        tile_copy(0, x, xs, i).start()
        tile_copy(1, dyb, dys, i).start()
    for copy in late[2:]:
        copy.start()
    small[...] = small_a[...]
    late[0].wait()
    late[1].wait()

    hidden = w1.shape[1]

    @pl.loop(0, tiles)
    def _(i):
        at = pl.ds(pl.multiple_of(i * WIDE, WIDE), WIDE)
        tile_copy(0, x, xs, i).wait()
        tile_copy(1, dyb, dys, i).wait()
        xhat, _ = normed(xs[at, :].astype(f32))
        h2s[at, :] = (xhat * gain_ref[1:2, :] + bias_ref[1:2, :]).astype(bf16)
        for c in range(2):
            wide = slice(c * (hidden // 2), (c + 1) * (hidden // 2))
            pre = dot_nn(h2s[at, :], w1s[:, wide]) + as_line(fb_ref[...])[:, wide]
            da = dot_nn(dys[at, :], w2s[:, wide])
            act, slope = gelu_both(pre)
            acts[at, wide] = act.astype(bf16)
            dab = (da * slope).astype(bf16)
            dabs[at, wide] = dab
            small[6:7, wide] += jnp.sum(dab.astype(f32), axis=0, keepdims=True)

    for copy in late[2:5]:
        copy.wait()
    base = 0
    for left, right in ((h1s, ps), (cs, dys), (h2s, dabs), (acts, dys)):
        tall = min(WIDE, left.shape[1])
        jobs, per_row = left.shape[1] // tall, right.shape[1] // BLOCK
        blocks = tall // BLOCK * per_row

        @pl.loop(0, jobs)
        def _(j):
            found = dot_tn(left[:, pl.ds(pl.multiple_of(j * tall, tall), tall)], right[...]).astype(bf16)
            start = base + j * blocks
            for r in range(tall // BLOCK):
                for c in range(per_row):
                    gs[start + r * per_row + c] = found[
                        r * BLOCK : (r + 1) * BLOCK, c * BLOCK : (c + 1) * BLOCK
                    ]

        base += jobs * blocks

    pl.semaphore_wait(barrier, 3 + count - 1)
    pl.semaphore_signal(free, inc=1, device_id=(me, near), device_id_type=MESH)
    scatter = Scatter(ring, order, gs, grad, sbuf, rbuf, ss, sr)
    kept = (h2s, dys)
    sums = [RowSum(kept[n], h1s, 2 * n, r2.at[n], rs.at[n], rr.at[n]) for n in range(2)]

    def t_copy(step):
        return pltpu.make_async_remote_copy(
            src_ref=small, dst_ref=t_in.at[tensor], send_sem=ts.at[step], recv_sem=tr.at[step],
            device_id=(me, (tensor + step) % 4), device_id_type=MESH,
        )

    def d_copy(step):
        return pltpu.make_async_remote_copy(
            src_ref=d_out, dst_ref=d_in.at[me], send_sem=ds.at[step], recv_sem=dr.at[step],
            device_id=((me + step) % count, tensor), device_id_type=MESH,
        )

    far = count // 2
    first, second = ((0, 0), (1, 1)), ((1, 0), (0, 1))
    for half, way in first + second:
        if hop_count(half, way, count) >= 1:
            scatter.step(half, way, 1, True)

    def ring_step(hop, which):
        for half, way in which:
            if which is first:
                scatter.step(half, way, hop, False)
            else:

                @pl.when(hop <= far - 1)
                def _():
                    scatter.step(half, way, hop, False)

    wide, thin = 6 * HEAD, 2 * HEAD
    total = lambda v: jnp.sum(v, axis=0, keepdims=True)

    def work(n, r):
        owner = (near * (1 - n % 2) + tensor * (n % 2) + 2 * (1 - n // 2)) % 4
        at = pl.ds(pl.multiple_of(owner * rows + r * TILE, TILE), TILE)
        to = pl.ds(pl.multiple_of(n * rows + r * TILE, TILE), TILE)
        br = dot_nt(acts[at, :], w2s[...])
        dh1 = None
        for p in range(2):
            lo = p * (wide + thin)
            br = br + dot_nt(cs[at, p * thin : (p + 1) * thin], wqds[:, lo + wide : lo + wide + thin])
            part = dot_nt(ps[at, p * wide : (p + 1) * wide], wqds[:, lo : lo + wide])
            dh1 = part if dh1 is None else dh1 + part
        kept[0][to, :] = br.astype(bf16)
        dh2 = dot_nt(dabs[at, :], w1s[...])
        xhat, _ = normed(xs[at, :].astype(f32))
        kept[1][to, :] = (dh1 * gain_ref[0:1, :] + dh2 * gain_ref[1:2, :]).astype(bf16)
        small[0:1, :] += total(dh1 * xhat)
        small[1:2, :] += total(dh2 * xhat)
        small[2:3, :] += total(dh1)
        small[3:4, :] += total(dh2)

    late[5].wait()
    @pl.loop(0, 4)
    def _(n):
        @pl.loop(0, rows // TILE)
        def _(r):
            work(n, r)

        @pl.when(n == 0)
        def _():
            pl.semaphore_wait(free, 1)
            for s in sums:
                s.pair(0).start()

        @pl.when(n == 1)
        def _():
            for s in sums:
                s.middle()
            sums[0].cross().start()
            if far >= 2 and count <= 8:
                ring_step(2, first)

        @pl.when(n == 2)
        def _():
            for s in sums:
                s.pair(1).start()

        @pl.when(n == 3)
        def _():
            if far >= 2 and count <= 8:
                ring_step(2, second)

    for step in range(1, 4):
        t_copy(step).start()
    sums[1].cross().start()

    def both(hop):
        ring_step(hop, first)
        ring_step(hop, second)

    if count <= 8:
        both(3)
    else:
        for_hops(2, far + 1, both, count)
    for step in range(1, 4):
        t_copy(step).wait_recv()
    t_in[tensor] = small[...]
    row = lax.broadcasted_iota(jnp.int32, small.shape, 0)
    summed = t_in[0] + t_in[1] + t_in[2] + t_in[3]
    d_out[...] = jnp.where(row < 4, summed, small[...])

    @pl.loop(1, count)
    def _(step):
        d_copy(step).start()

    if count <= 8:
        both(4)
    sums[0].end(stage, br_out, os)

    @pl.loop(1, count)
    def _(step):
        d_copy(step).wait_recv()

    d_in[me] = d_out[...]
    small_sum[...] = scale * lax.fori_loop(1, count, lambda k, acc: acc + d_in[k], d_in[0])
    sums[1].end(stage, e_out, os)
    for half in range(2):
        scatter.last(half, scale)
    scatter.finish()
    for s in sums:
        s.finish()
    for step in range(1, 4):
        t_copy(step).wait_send()

    @pl.loop(1, count)
    def _(step):
        d_copy(step).wait_send()


def tail_all(count, scale, order, gains, biases, fc1_bias, small, x, h1, dyb, ctx, dproj, wqd, w1, w2):
    rows, width = x.shape[0] // 4, x.shape[1]
    hidden = w1.shape[1]
    blocks = (width * (dproj.shape[1] + hidden) + (ctx.shape[1] + hidden) * width) // (BLOCK * BLOCK)
    per = blocks // count
    far = count // 2
    any_, vmem = pl.BlockSpec(memory_space=pl.ANY), pl.BlockSpec(memory_space=pltpu.VMEM)
    dma = lambda *n: pltpu.SemaphoreType.DMA(n)
    like = lambda v: pltpu.VMEM(v.shape, v.dtype)
    sum_shape = jax.ShapeDtypeStruct((rows, width), f32)
    tall = lambda cols: pltpu.VMEM((x.shape[0], cols), bf16)
    return pl.pallas_call(
        functools.partial(tail_kernel, count, scale),
        out_shape=[
            jax.ShapeDtypeStruct((per, BLOCK, BLOCK), f32), jax.ShapeDtypeStruct(small.shape, f32),
            sum_shape, sum_shape,
        ],
        in_specs=[pl.BlockSpec(memory_space=pltpu.SMEM)] + [vmem] * 4 + [any_] * 8,
        out_specs=[vmem, vmem, any_, any_],
        scratch_shapes=[like(v) for v in (x, h1, dyb, ctx, dproj, wqd, w1, w2)]
        + [
            tall(width), tall(hidden), tall(hidden), pltpu.VMEM((blocks, BLOCK, BLOCK), bf16),
            pltpu.VMEM((4, per, 64, BLOCK), bf16), pltpu.VMEM((4 * far, per, 64, BLOCK), bf16),
            pltpu.VMEM((2, rows, width), bf16), pltpu.VMEM((2, 64, width), f32),
            pltpu.VMEM(small.shape, f32), pltpu.VMEM((4,) + small.shape, f32),
            pltpu.VMEM((count,) + small.shape, f32), pltpu.VMEM(small.shape, f32),
            dma(2, x.shape[0] // WIDE), dma(6),
            dma(4 * far), dma(4 * far), dma(2, 3), dma(2, 3), dma(4), dma(4), dma(count), dma(count),
            dma(2), pltpu.SemaphoreType.REGULAR,
        ],
        compiler_params=pltpu.CompilerParams(
            collective_id=1, has_side_effects=True, vmem_limit_bytes=VMEM_LIMIT
        ),
        cost_estimate=pl.CostEstimate(flops=int(3.5e10), bytes_accessed=int(4e7), transcendentals=int(4e6)),
        name="tail_all",
    )(order, gains, biases, fc1_bias, small, x, h1, dyb, ctx, dproj, wqd, w1, w2)


def finish_kernel(
    steps, lim_ref, bias_ref, small_ref, racc_ref, qacc_ref, facc_ref, grad, tok, dy, br, e, ls, rs, lr, rr,
    gout, out, dx, lout, rout, cout, racc, rupd, qacc, qupd, facc, fupd,
    g_v, tok_v, dy_v, br_v, e_v, ls_v, rs_v, lr_v, rr_v, out_v, dx_v, lo_v, ro_v, co_v, isem, osem,
):
    tensor = lax.axis_index("tensor")
    own_rows, blocks = tok.shape[0], grad.shape[0]
    rows, some = own_rows // steps, blocks // steps
    ins = [(grad, g_v), (ls, ls_v), (rs, rs_v), (lr, lr_v), (rr, rr_v), (tok, tok_v), (dy, dy_v), (br, br_v), (e, e_v)]
    outs = [(g_v, gout), (lo_v, lout), (ro_v, rout), (co_v, cout), (out_v, out), (dx_v, dx)]

    def span(ref, s):
        size = ref.shape[0] // steps
        return ref.at[pl.ds(s * size if ref.shape[0] == blocks else pl.multiple_of(s * size, 16), size)]

    def fetch(k, s):
        return pltpu.make_async_copy(span(ins[k][0], s), span(ins[k][1], s), isem.at[k, s])

    def store(k, s):
        return pltpu.make_async_copy(span(outs[k][0], s), span(outs[k][1], s), osem.at[k, s])

    for s in range(steps):
        for k in range(len(ins)):
            fetch(k, s).start()
    small = small_ref[...]

    def adagrad(grad_vec, accum, new, update):
        accum_next = accum + grad_vec * grad_vec
        new[...] = accum_next
        update[...] = -adagrad_rate * grad_vec * lax.rsqrt(accum_next)

    def stacked(line, count):
        return jnp.concatenate([line[:, k * BLOCK : (k + 1) * BLOCK] for k in range(count)], axis=0)

    adagrad(jnp.concatenate([small[0:5], small[4:5]], axis=0), racc_ref[...], racc, rupd)
    adagrad(stacked(small[5:6], qacc.shape[0]), qacc_ref[...], qacc, qupd)
    adagrad(stacked(small[6:7], facc.shape[0]), facc_ref[...], facc, fupd)
    shift = bias_ref[2:3, :] + bias_ref[3:4, :]

    @pl.loop(0, steps)
    def _(s):
        for k in range(len(ins)):
            fetch(k, s).wait()

        for b in range(some):
            k = s * some + b
            low = g_v[k].astype(bf16)
            lo_v[k] = stat_decay * ls_v[k] + (1.0 - stat_decay) * dot_nt(low, low)
            ro_v[k] = stat_decay * rs_v[k] + (1.0 - stat_decay) * dot_tn(low, low)
            pushed = dot_nn(lr_v[k].astype(bf16), low).astype(bf16)
            co_v[k] = -shampoo_rate * dot_nn(pushed, rr_v[k].astype(bf16))

        at = pl.ds(pl.multiple_of(s * rows, 16), rows)
        x = tok_v[at, :].astype(f32)
        out_v[at, :] = (x + br_v[at, :] + shift).astype(bf16)
        start = tensor * own_rows + s * rows
        place = start % LEN + lax.broadcasted_iota(jnp.int32, (rows, 1), 0)
        kept = jnp.where(place < lim_ref[start // LEN], dy_v[at, :].astype(f32), 0.0)
        xhat, scale = normed(x)
        v = e_v[at, :]
        dx_v[at, :] = kept + scale * (
            v - jnp.mean(v, axis=-1, keepdims=True) - xhat * jnp.mean(v * xhat, axis=-1, keepdims=True)
        )
        for k in range(len(outs)):
            store(k, s).start()

    for s in range(steps):
        for k in range(len(outs)):
            store(k, s).wait()


def finish_all(limits, biases, small, racc, qacc, facc, grad, tok, dy, br, e, ls, rs, lr, rr):
    steps = 4 if grad.shape[0] % 4 == 0 else 1
    any_, vmem = pl.BlockSpec(memory_space=pl.ANY), pl.BlockSpec(memory_space=pltpu.VMEM)
    shape = lambda v: jax.ShapeDtypeStruct(v.shape, v.dtype)
    like = lambda v: pltpu.VMEM(v.shape, v.dtype)
    vectors = [racc, racc, qacc, qacc, facc, facc]
    return pl.pallas_call(
        functools.partial(finish_kernel, steps),
        out_shape=[shape(grad), shape(tok), shape(e)] + [shape(grad)] * 3 + [shape(v) for v in vectors],
        in_specs=[pl.BlockSpec(memory_space=pltpu.SMEM)] + [vmem] * 5 + [any_] * 9,
        out_specs=[any_] * 6 + [vmem] * 6,
        scratch_shapes=[like(v) for v in (grad, tok, dy, br, e, ls, rs, lr, rr, tok, e, ls, ls, ls)]
        + [pltpu.SemaphoreType.DMA((9, steps)), pltpu.SemaphoreType.DMA((6, steps))],
        compiler_params=pltpu.CompilerParams(vmem_limit_bytes=VMEM_LIMIT),
        cost_estimate=pl.CostEstimate(flops=int(4e8), bytes_accessed=int(2e7), transcendentals=0),
        name="finish_all",
    )(limits, biases, small, racc, qacc, facc, grad, tok, dy, br, e, ls, rs, lr, rr)


def shards(
    tokens, out_grad, seq_lengths, norm_gains, row_biases, qkv_weight, qkv_bias, dense_weight, fc1_weight,
    fc1_bias, fc2_weight, block_slot, left_stat, right_stat, left_root, right_root, row_accum,
    qkv_bias_accum, fc1_bias_accum,
):
    tensor_count = lax.axis_size("tensor")
    dp_count = lax.axis_size("dp")
    grad_scale = 1.0 / math.sqrt(tokens.shape[0] * tensor_count * dp_count)
    xf, h1, dyb, ctx, dproj, wqdf, w1f, w2f, sum_a, order = mixed_all(
        dp_count, seq_lengths, norm_gains, row_biases, as_rows(qkv_bias), jnp.asarray(rotary_rows()),
        as_rows(block_slot), tokens, out_grad, qkv_weight, dense_weight, fc1_weight, fc2_weight,
    )
    own_grad, small, branch, e_sum = tail_all(
        dp_count, grad_scale, order, norm_gains, row_biases, as_rows(fc1_bias), sum_a,
        xf, h1, dyb, ctx, dproj, wqdf, w1f, w2f,
    )
    outs = finish_all(
        seq_lengths, row_biases, small, row_accum, as_rows(qkv_bias_accum), as_rows(fc1_bias_accum),
        own_grad, tokens, out_grad, branch, e_sum, left_stat, right_stat, left_root, right_root,
    )
    block_grad, layer_out, input_grad, left_new, right_new, change = outs[:6]
    return (
        layer_out, input_grad, block_grad, left_new, right_new, change,
        *outs[6:8], *(v.reshape(-1) for v in outs[8:]),
    )


def solution(mesh):
    both = ("dp", "tensor")
    return jax.shard_map(
        shards,
        mesh=mesh,
        in_specs=(
            P(both, None), P(both, None), P("dp"), P(), P(), P("dp", "tensor"), P("tensor"),
            P("tensor", "dp"), P("dp", "tensor"), P("tensor"), P("tensor", "dp"), P(),
            P(both, None, None), P(both, None, None), P(both, None, None), P(both, None, None),
            P(), P("tensor"), P("tensor"),
        ),
        out_specs=(
            P(both, None), P(both, None), P(both, None, None), P(both, None, None),
            P(both, None, None), P(both, None, None), P(), P(), P("tensor"), P("tensor"),
            P("tensor"), P("tensor"),
        ),
        check_vma=False,
    )
```

profile of v0, /device:TPU:0, one launch (start us, length us, event | category | flops | bytes accessed | tf_op | source)
XLA Modules:
  0.0 189.9 jit_solution(12384126043619644507)
XLA Ops:
  0.6 74.0 %mixed_all.1 = (bf16[2048,1024]{1,0:T(8,128)(2,1)}, bf16[2048,1024]{1,0:T(8,128)(2,1)}, bf16[2048,1024]{1,0:T(8,128)(2,1)}, bf16[2048,256]{1,0:T(8,128)(2,1)}, b...) custom-call(s32[2]{0:T(128)} %lim_ref.3, ...), custom_call_target="tpu_custom_call" | custom-call | flops 20000000000 | bytes 40000000 | tf_op jit(solution)/shard_map/mixed_all/pallas_call | solution.py:619
  74.7 103.1 %tail_all.1 = (f32[24,128,128]{2,1,0:T(8,128)}, f32[8,1024]{1,0:T(8,128)}, f32[512,1024]{1,0:T(8,128)}, f32[512,1024]{1,0:T(8,128)}) custom-call(s32[8,192]{1,0:T(8,128)} %get-tuple-element.38.order, f32[2,1024]{1,0:T(2,128)} %gain_ref.3, f32[4,1024]{1,0:T(4,128)} %bias_ref.5, f32[8,128]{1,0:T(8,128)} %bitcast.13, f32[8,1024]{1,0:T(8,128)} %get-tuple-element.39.small_a, ...), custom_call_target="tpu_custom_call" | custom-call | flops 35000000512 | bytes 40000000 | tf_op jit(solution)/shard_map/tail_all/pallas_call | solution.py:1000
  177.8 11.9 %finish_all.1 = (f32[24,128,128]{2,1,0:T(8,128)}, bf16[512,1024]{1,0:T(8,128)(2,1)}, f32[512,1024]{1,0:T(8,128)}, f32[24,128,128]{2,1,0:T(8,128)}, f32[24,128,12...) custom-call(s32[2]{0:T(128)} %lim_ref.3, ...), custom_call_target="tpu_custom_call" | custom-call | flops 400000000 | bytes 20000000 | tf_op jit(solution)/shard_map/finish_all/pallas_call | solution.py:1104
where the time goes:
time: 190 us
  Pallas kernels  189 us (99%)
    pallas_call x1, Pallas kernels, tail_all(): pl.pallas_call(functools.partial(tail_kernel, count, scale), out_shape=[j...  103 us
    pallas_call x1, Pallas kernels, mixed_all(): pl.pallas_call(functools.partial(mixed_kernel, count), out_shape=[out(row...  74 us
    pallas_call x1, Pallas kernels, finish_all(): pl.pallas_call(functools.partial(finish_kernel, steps), out_shape=[shape(...  11.9 us

commit v1 on v0

--- a/solution.py
+++ b/solution.py
@@ -643,13 +643,9 @@
 
 
 def gelu_both(x):
-    bell = jnp.exp(-0.5 * x * x)
-    u = jnp.abs(x) * (1.0 / math.sqrt(2.0))
-    t = 1.0 / (1.0 + 0.3275911 * u)
-    poly = t * (0.254829592 + t * (-0.284496736 + t * (1.421413741 + t * (-1.453152027 + t * 1.061405429))))
-    tail = 0.5 * poly * bell
-    phi = jnp.where(x < 0.0, tail, 1.0 - tail)
-    return x * phi, phi + x * bell * (1.0 / math.sqrt(2.0 * math.pi))
+    phi = 0.5 + 0.5 * lax.erf(x * (1.0 / math.sqrt(2.0)))
+    bell = jnp.exp(-0.5 * x * x) * (1.0 / math.sqrt(2.0 * math.pi))
+    return x * phi, phi + x * bell
 
 
 class Scatter:
@@ -657,6 +653,7 @@
         self.ring, self.order, self.blocks, self.out = ring, order, blocks, out
         self.sbuf, self.rbuf, self.send, self.recv = sbuf, rbuf, send, recv
         self.per = out.shape[0]
+        self.together = 6 if self.per % 6 == 0 else 1
         self.far = ring.count // 2
 
     def index(self, half, way, hop):
@@ -674,7 +671,7 @@
         )
 
     def own(self, dest, half, k):
-        return self.blocks[self.order[0, dest * self.per + k], half * 64 : half * 64 + 64, :].astype(f32)
+        return self.blocks[self.order[0, dest * self.per + k], half * 64 : half * 64 + 64, :]
 
     def step(self, half, way, hop, first):
         hops = hop_count(half, way, self.ring.count)
@@ -686,12 +683,12 @@
         def one(k, carry):
             value = self.own(dest, half, k)
             if first:
-                self.sbuf[half * 2 + way, k] = value.astype(bf16)
+                self.sbuf[half * 2 + way, k] = value
             else:
-                self.rbuf[i - 1, k] = (value + self.rbuf[i - 1, k].astype(f32)).astype(bf16)
+                self.rbuf[i - 1, k] = (value.astype(f32) + self.rbuf[i - 1, k].astype(f32)).astype(bf16)
             return carry
 
-        lax.fori_loop(0, self.per, one, 0)
+        lax.fori_loop(0, self.per, one, 0, unroll=self.together)
         self.copy(half, way, hop, first).start()
 
     def last(self, half, scale):
@@ -704,13 +701,13 @@
         me = self.ring.me
 
         def one(k, carry):
-            value = self.own(me, half, k)
+            value = self.own(me, half, k).astype(f32)
             for i in came:
                 value = value + self.rbuf[i, k].astype(f32)
             self.out[k, half * 64 : half * 64 + 64, :] = value * scale
             return carry
 
-        lax.fori_loop(0, self.per, one, 0)
+        lax.fori_loop(0, self.per, one, 0, unroll=self.together)
 
     def finish(self):
         for half in range(2):

time: 190 us -> 187 us (0.984)
  Pallas kernels: 189 us -> 186 us
    pallas_call x1, Pallas kernels: 103 us -> 99.9 us  [tail_all(): pl.pallas_call(functools.partial(tail_kernel, count, scale), out_shape=[j...]
where the time goes in v1:
time: 187 us
  Pallas kernels  186 us (99%)
    pallas_call x1, Pallas kernels, tail_all(): pl.pallas_call(functools.partial(tail_kernel, count, scale), out_shape=[j...  99.9 us
    pallas_call x1, Pallas kernels, mixed_all(): pl.pallas_call(functools.partial(mixed_kernel, count), out_shape=[out(row...  74 us
    pallas_call x1, Pallas kernels, finish_all(): pl.pallas_call(functools.partial(finish_kernel, steps), out_shape=[shape(...  11.9 us

profile of v1, /device:TPU:0, one launch (start us, length us, event | category | flops | bytes accessed | tf_op | source)
XLA Modules:
  0.0 186.7 jit_solution(6752086580095120805)
XLA Ops:
  0.6 74.0 %mixed_all.1 = (bf16[2048,1024]{1,0:T(8,128)(2,1)}, bf16[2048,1024]{1,0:T(8,128)(2,1)}, bf16[2048,1024]{1,0:T(8,128)(2,1)}, bf16[2048,256]{1,0:T(8,128)(2,1)}, b...) custom-call(s32[2]{0:T(128)} %lim_ref.3, ...), custom_call_target="tpu_custom_call" | custom-call | flops 20000000000 | bytes 40000000 | tf_op jit(solution)/shard_map/mixed_all/pallas_call | solution.py:619
  74.7 99.9 %tail_all.1 = (f32[24,128,128]{2,1,0:T(8,128)}, f32[8,1024]{1,0:T(8,128)}, f32[512,1024]{1,0:T(8,128)}, f32[512,1024]{1,0:T(8,128)}) custom-call(s32[8,192]{1,0:T(8,128)} %get-tuple-element.38.order, f32[2,1024]{1,0:T(2,128)} %gain_ref.3, f32[4,1024]{1,0:T(4,128)} %bias_ref.5, f32[8,128]{1,0:T(8,128)} %bitcast.13, f32[8,1024]{1,0:T(8,128)} %get-tuple-element.39.small_a, ...), custom_call_target="tpu_custom_call" | custom-call | flops 35000000512 | bytes 40000000 | tf_op jit(solution)/shard_map/tail_all/pallas_call | solution.py:997
  174.6 11.9 %finish_all.1 = (f32[24,128,128]{2,1,0:T(8,128)}, bf16[512,1024]{1,0:T(8,128)(2,1)}, f32[512,1024]{1,0:T(8,128)}, f32[24,128,128]{2,1,0:T(8,128)}, f32[24,128,12...) custom-call(s32[2]{0:T(128)} %lim_ref.3, ...), custom_call_target="tpu_custom_call" | custom-call | flops 400000000 | bytes 20000000 | tf_op jit(solution)/shard_map/finish_all/pallas_call | solution.py:1101

commit v2 on v1

--- a/solution.py
+++ b/solution.py
@@ -473,10 +473,10 @@
     ry.keep().wait()
     ry.pair().wait_recv()
 
-    @pl.loop(0, tiles // 2)
+    @pl.loop(0, tiles // 4)
     def _(i):
-        for sub in range(2):
-            prepare_tile(seq, 0, 2 * i + sub)
+        for sub in range(4):
+            prepare_tile(seq, 0, 4 * i + sub)
 
 
     @pl.loop(0, tiles)
@@ -493,11 +493,11 @@
             hop_at(1, 4)
             hop_at(2, 1)
 
-            @pl.loop(0, tiles // 2)
+            @pl.loop(0, tiles // 4)
             def _(i):
-                for sub in range(2):
-                    prepare_tile(seq, 1, 2 * i + sub)
-                    context_tile(seq, 1, 2 * i + sub)
+                for sub in range(4):
+                    prepare_tile(seq, 1, 4 * i + sub)
+                    context_tile(seq, 1, 4 * i + sub)
 
         attend(pair, 3, (0, 1, 2, 3))
 
@@ -543,10 +543,10 @@
 
     for pair in range(2):
 
-        @pl.loop(0, tiles // 2)
+        @pl.loop(0, tiles // 4)
         def _(i):
-            for sub in range(2):
-                prepare_tile(seq, pair, 2 * i + sub)
+            for sub in range(4):
+                prepare_tile(seq, pair, 4 * i + sub)
 
         if pair == 0:
             hop_at(2, 2)
@@ -818,8 +818,8 @@
         tile_copy(1, dyb, dys, i).wait()
         xhat, _ = normed(xs[at, :].astype(f32))
         h2s[at, :] = (xhat * gain_ref[1:2, :] + bias_ref[1:2, :]).astype(bf16)
-        for c in range(2):
-            wide = slice(c * (hidden // 2), (c + 1) * (hidden // 2))
+        for c in range(1):
+            wide = slice(0, hidden)
             pre = dot_nn(h2s[at, :], w1s[:, wide]) + as_line(fb_ref[...])[:, wide]
             da = dot_nn(dys[at, :], w2s[:, wide])
             act, slope = gelu_both(pre)
@@ -1093,7 +1093,7 @@
 
 
 def finish_all(limits, biases, small, racc, qacc, facc, grad, tok, dy, br, e, ls, rs, lr, rr):
-    steps = 4 if grad.shape[0] % 4 == 0 else 1
+    steps = 8 if grad.shape[0] % 8 == 0 else 1
     any_, vmem = pl.BlockSpec(memory_space=pl.ANY), pl.BlockSpec(memory_space=pltpu.VMEM)
     shape = lambda v: jax.ShapeDtypeStruct(v.shape, v.dtype)
     like = lambda v: pltpu.VMEM(v.shape, v.dtype)

time: 187 us -> 183 us (0.979)
  Pallas kernels: 186 us -> 182 us
    pallas_call x1, Pallas kernels: 99.9 us -> 97.6 us  [tail_all(): pl.pallas_call(functools.partial(tail_kernel, count, scale), out_shape=[j...]
where the time goes in v2:
time: 183 us
  Pallas kernels  182 us (99%)
    pallas_call x1, Pallas kernels, tail_all(): pl.pallas_call(functools.partial(tail_kernel, count, scale), out_shape=[j...  97.6 us
    pallas_call x1, Pallas kernels, mixed_all(): pl.pallas_call(functools.partial(mixed_kernel, count), out_shape=[out(row...  72.9 us
    pallas_call x1, Pallas kernels, finish_all(): pl.pallas_call(functools.partial(finish_kernel, steps), out_shape=[shape(...  11.4 us

profile of v2, /device:TPU:0, one launch (start us, length us, event | category | flops | bytes accessed | tf_op | source)
XLA Modules:
  0.0 182.7 jit_solution(4037379869598501666)
XLA Ops:
  0.6 72.9 %mixed_all.1 = (bf16[2048,1024]{1,0:T(8,128)(2,1)}, bf16[2048,1024]{1,0:T(8,128)(2,1)}, bf16[2048,1024]{1,0:T(8,128)(2,1)}, bf16[2048,256]{1,0:T(8,128)(2,1)}, b...) custom-call(s32[2]{0:T(128)} %lim_ref.3, ...), custom_call_target="tpu_custom_call" | custom-call | flops 20000000000 | bytes 40000000 | tf_op jit(solution)/shard_map/mixed_all/pallas_call | solution.py:619
  73.6 97.6 %tail_all.1 = (f32[24,128,128]{2,1,0:T(8,128)}, f32[8,1024]{1,0:T(8,128)}, f32[512,1024]{1,0:T(8,128)}, f32[512,1024]{1,0:T(8,128)}) custom-call(s32[8,192]{1,0:T(8,128)} %get-tuple-element.38.order, f32[2,1024]{1,0:T(2,128)} %gain_ref.3, f32[4,1024]{1,0:T(4,128)} %bias_ref.5, f32[8,128]{1,0:T(8,128)} %bitcast.13, f32[8,1024]{1,0:T(8,128)} %get-tuple-element.39.small_a, ...), custom_call_target="tpu_custom_call" | custom-call | flops 35000000512 | bytes 40000000 | tf_op jit(solution)/shard_map/tail_all/pallas_call | solution.py:997
  171.2 11.4 %finish_all.1 = (f32[24,128,128]{2,1,0:T(8,128)}, bf16[512,1024]{1,0:T(8,128)(2,1)}, f32[512,1024]{1,0:T(8,128)}, f32[24,128,128]{2,1,0:T(8,128)}, f32[24,128,12...) custom-call(s32[2]{0:T(128)} %lim_ref.3, ...), custom_call_target="tpu_custom_call" | custom-call | flops 400000000 | bytes 20000000 | tf_op jit(solution)/shard_map/finish_all/pallas_call | solution.py:1101

commit v3 on v2

--- a/solution.py
+++ b/solution.py
@@ -770,9 +770,9 @@
 
 def tail_kernel(
     count, scale, order, gain_ref, bias_ref, fb_ref, small_a, x, h1, dyb, ctx, dproj, wqd, w1, w2,
-    grad, small_sum, br_out, e_out,
-    xs, h1s, dys, cs, ps, wqds, w1s, w2s, h2s, acts, dabs, gs, sbuf, rbuf, r2, stage, small, t_in, d_in, d_out,
-    sem, late_sem, ss, sr, rs, rr, ts, tr, ds, dr, os, free,
+    grad_out, small_sum, br_out, e_out,
+    grad, xs, h1s, dys, cs, ps, wqds, w1s, w2s, h2s, acts, dabs, gs, sbuf, rbuf, r2, stage, small, t_in, d_in, d_out,
+    sem, late_sem, ss, sr, rs, rr, ts, tr, ds, dr, os, gsem, free,
 ):
     ring = Ring(count)
     me, tensor = ring.me, ring.tensor
@@ -970,8 +970,12 @@
     d_in[me] = d_out[...]
     small_sum[...] = scale * lax.fori_loop(1, count, lambda k, acc: acc + d_in[k], d_in[0])
     sums[1].end(stage, e_out, os)
+    parts_out = []
     for half in range(2):
         scatter.last(half, scale)
+        at = pl.ds(half * 64, 64)
+        parts_out.append(pltpu.make_async_copy(grad.at[:, at], grad_out.at[:, at], gsem.at[half]))
+        parts_out[-1].start()
     scatter.finish()
     for s in sums:
         s.finish()
@@ -981,6 +985,9 @@
     @pl.loop(1, count)
     def _(step):
         d_copy(step).wait_send()
+
+    for copy in parts_out:
+        copy.wait()
 
 
 def tail_all(count, scale, order, gains, biases, fc1_bias, small, x, h1, dyb, ctx, dproj, wqd, w1, w2):
@@ -1001,8 +1008,9 @@
             sum_shape, sum_shape,
         ],
         in_specs=[pl.BlockSpec(memory_space=pltpu.SMEM)] + [vmem] * 4 + [any_] * 8,
-        out_specs=[vmem, vmem, any_, any_],
-        scratch_shapes=[like(v) for v in (x, h1, dyb, ctx, dproj, wqd, w1, w2)]
+        out_specs=[any_, vmem, any_, any_],
+        scratch_shapes=[pltpu.VMEM((per, BLOCK, BLOCK), f32)]
+        + [like(v) for v in (x, h1, dyb, ctx, dproj, wqd, w1, w2)]
         + [
             tall(width), tall(hidden), tall(hidden), pltpu.VMEM((blocks, BLOCK, BLOCK), bf16),
             pltpu.VMEM((4, per, 64, BLOCK), bf16), pltpu.VMEM((4 * far, per, 64, BLOCK), bf16),
@@ -1011,7 +1019,7 @@
             pltpu.VMEM((count,) + small.shape, f32), pltpu.VMEM(small.shape, f32),
             dma(2, x.shape[0] // WIDE), dma(6),
             dma(4 * far), dma(4 * far), dma(2, 3), dma(2, 3), dma(4), dma(4), dma(count), dma(count),
-            dma(2), pltpu.SemaphoreType.REGULAR,
+            dma(2), dma(2), pltpu.SemaphoreType.REGULAR,
         ],
         compiler_params=pltpu.CompilerParams(
             collective_id=1, has_side_effects=True, vmem_limit_bytes=VMEM_LIMIT

time: 183 us -> 183 us (level)
  no operation moved by 1% of the time
where the time goes in v3:
time: 183 us
  Pallas kernels  182 us (99%)
    pallas_call x1, Pallas kernels, tail_all(): pl.pallas_call(functools.partial(tail_kernel, count, scale), out_shape=[j...  97.9 us
    pallas_call x1, Pallas kernels, mixed_all(): pl.pallas_call(functools.partial(mixed_kernel, count), out_shape=[out(row...  72.9 us
    pallas_call x1, Pallas kernels, finish_all(): pl.pallas_call(functools.partial(finish_kernel, steps), out_shape=[shape(...  11.4 us

profile of v3, /device:TPU:0, one launch (start us, length us, event | category | flops | bytes accessed | tf_op | source)
XLA Modules:
  0.0 183.0 jit_solution(8312151887560455862)
XLA Ops:
  0.6 72.9 %mixed_all.1 = (bf16[2048,1024]{1,0:T(8,128)(2,1)}, bf16[2048,1024]{1,0:T(8,128)(2,1)}, bf16[2048,1024]{1,0:T(8,128)(2,1)}, bf16[2048,256]{1,0:T(8,128)(2,1)}, b...) custom-call(s32[2]{0:T(128)} %lim_ref.3, ...), custom_call_target="tpu_custom_call" | custom-call | flops 20000000000 | bytes 40000000 | tf_op jit(solution)/shard_map/mixed_all/pallas_call | solution.py:619
  73.6 97.9 %tail_all.1 = (f32[24,128,128]{2,1,0:T(8,128)}, f32[8,1024]{1,0:T(8,128)}, f32[512,1024]{1,0:T(8,128)}, f32[512,1024]{1,0:T(8,128)}) custom-call(s32[8,192]{1,0:T(8,128)} %get-tuple-element.38.order, f32[2,1024]{1,0:T(2,128)} %gain_ref.3, f32[4,1024]{1,0:T(4,128)} %bias_ref.5, f32[8,128]{1,0:T(8,128)} %bitcast.13, f32[8,1024]{1,0:T(8,128)} %get-tuple-element.39.small_a, ...), custom_call_target="tpu_custom_call" | custom-call | flops 35000000512 | bytes 40000000 | tf_op jit(solution)/shard_map/tail_all/pallas_call | solution.py:1004
  171.4 11.4 %finish_all.1 = (f32[24,128,128]{2,1,0:T(8,128)}, bf16[512,1024]{1,0:T(8,128)(2,1)}, f32[512,1024]{1,0:T(8,128)}, f32[24,128,128]{2,1,0:T(8,128)}, f32[24,128,12...) custom-call(s32[2]{0:T(128)} %lim_ref.3, ...), custom_call_target="tpu_custom_call" | custom-call | flops 400000000 | bytes 20000000 | tf_op jit(solution)/shard_map/finish_all/pallas_call | solution.py:1109
